TPU v7x, 32 devices: a whole 2x2x4 slice. The times are simulated.
32 devices in a mesh: groups: 2 (over x), dev: 16 (over z, y, core).
Axes of the slice: x: 2, y: 2, z: 4, core: 2. Of those that a mesh axis runs over, the one named last changes fastest.
Arguments:
- inputs: bfloat16 [8192, 4096], P(('groups', 'dev')), parts along dimension 0, may hold values from -6 to 6
- query_cot: bfloat16 [8192, 4096], P(('groups', 'dev')), parts along dimension 0, may hold values from -0.59765625 to 0.59765625
- value_cot: bfloat16 [8192, 1024], P(('groups', 'dev')), parts along dimension 0, may hold values from -0.59765625 to 0.59765625
- block_adapter: int32 [64, 1], P(('groups', 'dev')), parts along dimension 0, may hold values from 0 to 15
- query_down: bfloat16 [32, 64, 4096], P(('groups', 'dev')), parts along dimension 0, may hold values from -0.09375 to 0.09375
- query_up: bfloat16 [32, 64, 4096], P(('groups', 'dev')), parts along dimension 0, may hold values from -0.75 to 0.75
- value_down: bfloat16 [32, 64, 4096], P(('groups', 'dev')), parts along dimension 0, may hold values from -0.09375 to 0.09375
- value_up: bfloat16 [32, 64, 1024], P(('groups', 'dev')), parts along dimension 0, may hold values from -0.75 to 0.75
Outputs:
- input_grad: bfloat16 [8192, 4096], P(('groups', 'dev')), parts along dimension 0
- qdown_grad: bfloat16 [32, 64, 4096], P(('groups', 'dev')), parts along dimension 0
- qup_grad: bfloat16 [32, 64, 4096], P(('groups', 'dev')), parts along dimension 0
- vdown_grad: bfloat16 [32, 64, 4096], P(('groups', 'dev')), parts along dimension 0
- vup_grad: bfloat16 [32, 64, 1024], P(('groups', 'dev')), parts along dimension 0
There are 2 independent parts, one for each index of `groups`. A program takes and returns all parts, laid end to end along the dimension named above; each array names one. Nothing has to cross between parts.
Inputs may be any that keep to these rules, and one draw needn't show every extreme that they name: `block_adapter`: every adapter is named by some block.
All inputs are finite; a program needn't handle non-finite values.
Results may differ from a plain program's by a relative error of at most 0.0058.
Values may be sent and summed in bfloat16 or wider, within the bound.
A program may use at most 64 MiB of HBM per device.

v0:
```python
import functools

import jax
import jax.numpy as jnp
from jax import lax
from jax.experimental import pallas as pl
from jax.experimental.pallas import tpu as pltpu
from jax.sharding import PartitionSpec as P

BLOCK = 128
ROWS = 16
LANES = 128
QD, VD, QU, VU = range(4)

adapter_scale = 2.0


def dot(left, right, dims):
    return lax.dot_general(left, right, (dims, ((), ())), preferred_element_type=jnp.float32)


def kernel(
    n, rank, per_dev, widths,
    ids_ref, x_ref, qc_ref, vc_ref, qd_ref, vd_ref, qu_ref, vu_ref,
    grad_ref, oqd_ref, ovd_ref, oqu_ref, ovu_ref,
    ids_v, ids_s, prev_s, last_s,
    hold_qd, hold_vd, hold_qu, hold_vu,
    stage_qd, stage_vd, stage_qu, stage_vu,
    tile_d, tile_qu, tile_vu, term_d, term_qu, term_vu,
    recv_qd, recv_vd, recv_qu, recv_vu,
    sum_qd, sum_vd, sum_qu, sum_vu,
    chain, chain_v, back_s,
    send_sem, recv_sem, id_send, id_recv, own_sem,
):
    group, me = lax.axis_index("groups"), lax.axis_index("dev")
    row_groups = rank // ROWS
    column_groups = n // row_groups
    share = [w // column_groups for w in widths]
    own = (qd_ref, vd_ref, qu_ref, vu_ref)
    out = (oqd_ref, ovd_ref, oqu_ref, ovu_ref)
    hold = (hold_qd, hold_vd, hold_qu, hold_vu)
    stage = (stage_qd, stage_vd, stage_qu, stage_vu)
    tile = (tile_d, tile_d, tile_qu, tile_vu)
    term = (term_d, term_d, term_qu, term_vu)
    recv = (recv_qd, recv_vd, recv_qu, recv_vu)
    sums = (sum_qd, sum_vd, sum_qu, sum_vu)
    chains = (chain, chain, chain, chain_v)
    base = (0, rank, 0, 0)

    def peer_of(off):
        return lax.rem(me + off, n)

    def source_of(off):
        return lax.rem(me + n - off, n)

    def rows(d, start):
        return pl.ds(pl.multiple_of(lax.div(d, column_groups) * ROWS + start, ROWS), ROWS)

    def columns(d, c):
        return pl.ds(pl.multiple_of(lax.rem(d, column_groups) * share[c], LANES), share[c])

    def remote(src, dst, phase, c, off, peer):
        return pltpu.make_async_remote_copy(
            src_ref=src, dst_ref=dst,
            send_sem=send_sem.at[phase, c, off], recv_sem=recv_sem.at[phase, c, off],
            device_id=(group, peer), device_id_type=pl.DeviceIdType.MESH,
        )

    def source(phase, c, d):
        if phase == 0:
            return own[c].at[0, rows(d, 0), columns(d, c)]
        if phase == 1:
            return stage[c].at[d]
        if phase == 2:
            return term[c].at[:, rows(d, base[c]), columns(d, c)]
        return sums[c].at[d]

    def target(phase, c, d):
        if phase == 0:
            return hold[c].at[d]
        if phase == 1:
            return tile[c].at[:, rows(d, base[c]), columns(d, c)]
        if phase == 2:
            return recv[c].at[d]
        return out[c].at[0, rows(d, 0), columns(d, c)]

    def each_peer(body):
        def step(off, carry):
            body(off)
            return carry

        lax.fori_loop(1, n, step, 0)

    def send(phase, c):
        each_peer(
            lambda off: remote(
                source(phase, c, peer_of(off)), target(phase, c, me), phase, c, off, peer_of(off)
            ).start()
        )
        pltpu.make_async_copy(source(phase, c, me), target(phase, c, me), own_sem.at[phase, c]).start()

    def arrive(phase, c):
        pltpu.make_async_copy(source(phase, c, me), target(phase, c, me), own_sem.at[phase, c]).wait()
        each_peer(
            lambda off: remote(
                source(phase, c, me), target(phase, c, source_of(off)), phase, c, off, peer_of(off)
            ).wait_recv()
        )

    def drain(phase, c):
        each_peer(
            lambda off: remote(
                source(phase, c, peer_of(off)), target(phase, c, me), phase, c, off, peer_of(off)
            ).wait_send()
        )

    def id_copy(off, slot):
        return pltpu.make_async_remote_copy(
            src_ref=ids_ref, dst_ref=ids_v.at[slot],
            send_sem=id_send.at[off], recv_sem=id_recv.at[off],
            device_id=(group, peer_of(off)), device_id_type=pl.DeviceIdType.MESH,
        )

    barrier = pltpu.get_barrier_semaphore()
    each_peer(
        lambda off: pl.semaphore_signal(
            barrier, inc=1, device_id=(group, peer_of(off)), device_id_type=pl.DeviceIdType.MESH
        )
    )
    pl.semaphore_wait(barrier, n - 1)

    each_peer(lambda off: id_copy(off, me).start())
    for c in (QD, VD, QU, VU):
        send(0, c)
    ids_v[me] = ids_ref[...]
    each_peer(lambda off: id_copy(off, source_of(off)).wait_recv())
    fetch = pltpu.make_async_copy(ids_v, ids_s, id_recv.at[0])
    fetch.start()
    fetch.wait()

    def pick(c):
        def step(d, carry):
            for k in range(per_dev):
                stage[c][d, k] = hold[c][ids_s[d, k, 0]]
            return carry

        lax.fori_loop(0, n, step, 0)

    for c in (QD, VD, QU, VU):
        arrive(0, c)
        pick(c)
        send(1, c)

    blocks = n * per_dev

    def id_of(b):
        return ids_s[lax.div(b, per_dev), lax.rem(b, per_dev), 0]

    def find_prev(b, carry):
        mine = id_of(b)
        prev_s[b] = lax.fori_loop(
            0, b, lambda j, found: jnp.where(id_of(j) == mine, j + 1, found), jnp.int32(0)
        )
        return carry

    lax.fori_loop(0, blocks, find_prev, 0)

    def find_last(a, carry):
        last_s[a] = lax.fori_loop(
            0, blocks, lambda j, found: jnp.where(id_of(j) == a, j + 1, found), jnp.int32(0)
        )
        return carry

    lax.fori_loop(0, n, find_last, 0)

    def slabs(width):
        size = 512 if width % 512 == 0 else LANES
        return width // size, size

    def contract(tile_ref, k, token_ref):
        width = token_ref.shape[2]
        count, size = slabs(width)

        def step(i, total):
            cols = pl.ds(pl.multiple_of(i * size, LANES), size)
            return total + dot(tile_ref[k, :, cols], token_ref[k, :, cols], ((1,), (1,)))

        return lax.fori_loop(
            0, count, step, jnp.zeros((tile_ref.shape[1], BLOCK), jnp.float32)
        )

    def expand(left, token_ref, k, target_ref, scale):
        count, size = slabs(token_ref.shape[2])

        def step(i, carry):
            cols = pl.ds(pl.multiple_of(i * size, LANES), size)
            value = dot(left, token_ref[k, :, cols], ((1,), (0,)))
            if scale is not None:
                value = scale * value
            target_ref[k, :, cols] = value.astype(jnp.bfloat16)
            return carry

        lax.fori_loop(0, count, step, 0)

    arrive(1, QD)
    arrive(1, VD)
    for k in range(per_dev):
        low = contract(tile_d, k, x_ref).astype(jnp.bfloat16)
        expand(low[:rank], qc_ref, k, term_qu, adapter_scale)
        expand(low[rank:], vc_ref, k, term_vu, adapter_scale)
    send(2, QU)
    send(2, VU)
    arrive(1, QU)
    arrive(1, VU)
    for k in range(per_dev):
        back_s[k, :rank] = adapter_scale * contract(tile_qu, k, qc_ref)
        back_s[k, rank:] = adapter_scale * contract(tile_vu, k, vc_ref)
        expand(back_s[k].astype(jnp.bfloat16), x_ref, k, term_d, None)
    send(2, QD)
    send(2, VD)

    def reduce(c):
        s = chains[c]
        s[0] = jnp.zeros(s.shape[1:], jnp.float32)

        def step(b, carry):
            piece = recv[c][lax.div(b, per_dev), lax.rem(b, per_dev)].astype(jnp.float32)
            s[b + 1] = piece + s[prev_s[b]]
            return carry

        lax.fori_loop(0, blocks, step, 0)

        def close(a, carry):
            sums[c][a] = s[last_s[a]].astype(jnp.bfloat16)
            return carry

        lax.fori_loop(0, n, close, 0)

    for c in (QU, VU):
        arrive(2, c)
        reduce(c)
        send(3, c)
    for k in range(per_dev):
        back = back_s[k].T.astype(jnp.bfloat16)
        expand(back, tile_d, k, grad_ref, None)
    for c in (QD, VD):
        arrive(2, c)
        reduce(c)
        send(3, c)
    each_peer(lambda off: id_copy(off, me).wait_send())
    for phase in range(3):
        for c in range(4):
            drain(phase, c)
    for c in (QU, VU, QD, VD):
        arrive(3, c)
        drain(3, c)


def per_device(
    inputs, query_cot, value_cot, block_adapter, query_down, query_up, value_down, value_up
):
    n = lax.axis_size("dev")
    rows, width = inputs.shape
    per_dev = rows // BLOCK
    rank = query_down.shape[1]
    column_groups = n // (rank // ROWS)

    def padded(w):
        return column_groups * max(LANES, w // column_groups)

    def spread(a):
        w = a.shape[-1]
        if padded(w) == w:
            return a
        parts = a.reshape(a.shape[:-1] + (column_groups, w // column_groups))
        extra = padded(w) // column_groups - w // column_groups
        parts = jnp.pad(parts, [(0, 0)] * (parts.ndim - 1) + [(0, extra)])
        return parts.reshape(a.shape[:-1] + (padded(w),))

    def unspread(a, w):
        if a.shape[-1] == w:
            return a
        parts = a.reshape(a.shape[:-1] + (column_groups, -1))
        return parts[..., : w // column_groups].reshape(a.shape[:-1] + (w,))

    vwidth = value_cot.shape[1]
    value_up, value_cot = spread(value_up), spread(value_cot)
    vpad = value_cot.shape[1]
    qwidth = query_cot.shape[1]
    widths = (width, width, qwidth, vpad)
    share = [w // column_groups for w in widths]
    ids = jnp.pad(
        jnp.broadcast_to(block_adapter, (per_dev, LANES)), ((0, -per_dev % 8), (0, 0))
    )
    bf, f32 = jnp.bfloat16, jnp.float32
    blocks = n * per_dev
    scratch = [
        pltpu.VMEM((n,) + ids.shape, jnp.int32),
        pltpu.SMEM((n,) + ids.shape, jnp.int32),
        pltpu.SMEM((blocks,), jnp.int32),
        pltpu.SMEM((n,), jnp.int32),
    ]
    scratch += [pltpu.VMEM((n, ROWS, s), bf) for s in share]
    scratch += [pltpu.VMEM((n, per_dev, ROWS, s), bf) for s in share]
    for _ in range(2):
        scratch += [
            pltpu.VMEM((per_dev, 2 * rank, width), bf),
            pltpu.VMEM((per_dev, rank, qwidth), bf),
            pltpu.VMEM((per_dev, rank, vpad), bf),
        ]
    scratch += [pltpu.VMEM((n, per_dev, ROWS, s), bf) for s in share]
    scratch += [pltpu.VMEM((n, ROWS, s), bf) for s in share]
    scratch += [
        pltpu.VMEM((blocks + 1, ROWS, share[QU]), f32),
        pltpu.VMEM((blocks + 1, ROWS, share[VU]), f32),
        pltpu.VMEM((per_dev, 2 * rank, BLOCK), f32),
        pltpu.SemaphoreType.DMA((4, 4, n)),
        pltpu.SemaphoreType.DMA((4, 4, n)),
        pltpu.SemaphoreType.DMA((n,)),
        pltpu.SemaphoreType.DMA((n,)),
        pltpu.SemaphoreType.DMA((4, 4)),
    ]
    vmem = pl.BlockSpec(memory_space=pltpu.VMEM)
    grad, qdown, vdown, qup, vup = pl.pallas_call(
        functools.partial(kernel, n, rank, per_dev, widths),
        out_shape=(
            jax.ShapeDtypeStruct((per_dev, BLOCK, width), bf),
            jax.ShapeDtypeStruct((1, rank, width), bf),
            jax.ShapeDtypeStruct((1, rank, width), bf),
            jax.ShapeDtypeStruct((1, rank, qwidth), bf),
            jax.ShapeDtypeStruct((1, rank, vpad), bf),
        ),
        in_specs=[vmem] * 8,
        out_specs=[vmem] * 5,
        scratch_shapes=scratch,
        compiler_params=pltpu.CompilerParams(
            collective_id=0, has_side_effects=True, vmem_limit_bytes=52 * 1024 * 1024
        ),
    )(
        ids,
        inputs.reshape(per_dev, BLOCK, width),
        query_cot.reshape(per_dev, BLOCK, qwidth),
        value_cot.reshape(per_dev, BLOCK, vpad),
        query_down,
        value_down,
        query_up,
        value_up,
    )
    return (grad.reshape(rows, width), qdown, qup, vdown, unspread(vup, vwidth))


def solution(mesh):
    rows = P(("groups", "dev"), None)
    factors = P(("groups", "dev"), None, None)
    return jax.shard_map(
        per_device,
        mesh=mesh,
        in_specs=(rows, rows, rows, rows, factors, factors, factors, factors),
        out_specs=(rows, factors, factors, factors, factors),
        check_vma=False,
    )
```

profile of v0, /device:TPU:0, one launch (start us, length us, event | category | flops | bytes accessed | tf_op | source)
XLA Modules:
  0.0 241.8 jit_solution(12388764552660796467)
XLA Ops:
  0.6 0.7 pad.6
  1.3 0.1 pad.7.ids_ref
  1.4 0.0 copy-start
  1.4 0.9 copy-done
  2.3 233.3 %shard_map.119 = (bf16[2,128,4096]{2,1,0:T(8,128)(2,1)}, bf16[1,64,4096]{2,1,0:T(8,128)(2,1)S(1)}, bf16[1,64,4096]{2,1,0:T(8,128)(2,1)S(1)}, bf16[1,64,4096]{2,1,0:T(8,128)(2,1)S(1)}, bf16[1,64,1024]{2,1,0:T(8,128)(2,1)S(1)}) custom-call(s32[8,128]{1,0:T(8,128)S(1)} %pad.7.ids_ref, bf16[2,128,4096]{2,1,0:T(8,128)(2,1)} %bitcast.6, ...), custom_call_target="tpu_custom_call" | custom-call | tf_op jit(solution)/shard_map/pallas_call | solution.py:324
  235.6 3.1 %copy.18 = bf16[256,4096]{1,0:T(8,128)(2,1)} copy(bf16[256,4096]{1,0:T(8,128)(2,1)} %bitcast.5) | data formatting | bytes 4194304
  238.7 0.8 copy.19
  239.5 0.8 copy.20
  240.3 0.8 copy.21
  241.1 0.7 copy.22
Async XLA Ops:
  1.4 0.9 copy-start
where the time goes:
time: 244 us; the launch traced here: 242 us
  Pallas kernels  233 us (95%)
  local copies, waits for them, and re-layouts  7.8 us (3%)
    pallas_call x1, Pallas kernels, per_device(): pl.pallas_call(functools.partial(kernel, n, rank, per_dev, widths), out_s...  233 us
    unnamed x7, local copies, waits for them, and re-layouts  7.07 us

commit v1 on v0

--- a/solution.py
+++ b/solution.py
@@ -20,7 +20,7 @@
 
 
 def kernel(
-    n, rank, per_dev, widths,
+    n, half, rank, per_dev, widths,
     ids_ref, x_ref, qc_ref, vc_ref, qd_ref, vd_ref, qu_ref, vu_ref,
     grad_ref, oqd_ref, ovd_ref, oqu_ref, ovu_ref,
     ids_v, ids_s, prev_s, last_s,
@@ -29,12 +29,14 @@
     tile_d, tile_qu, tile_vu, term_d, term_qu, term_vu,
     recv_qd, recv_vd, recv_qu, recv_vu,
     sum_qd, sum_vd, sum_qu, sum_vu,
+    home_qd, home_vd, home_qu, home_vu,
     chain, chain_v, back_s,
     send_sem, recv_sem, id_send, id_recv, own_sem,
 ):
     group, me = lax.axis_index("groups"), lax.axis_index("dev")
     row_groups = rank // ROWS
-    column_groups = n // row_groups
+    column_groups = half // row_groups
+    side, spot = lax.div(me, half), lax.rem(me, half)
     share = [w // column_groups for w in widths]
     own = (qd_ref, vd_ref, qu_ref, vu_ref)
     out = (oqd_ref, ovd_ref, oqu_ref, ovu_ref)
@@ -44,17 +46,22 @@
     term = (term_d, term_d, term_qu, term_vu)
     recv = (recv_qd, recv_vd, recv_qu, recv_vu)
     sums = (sum_qd, sum_vd, sum_qu, sum_vu)
+    home = (home_qd, home_vd, home_qu, home_vu)
     chains = (chain, chain, chain, chain_v)
     base = (0, rank, 0, 0)
 
-    def peer_of(off):
+    def peer_of(phase, off):
+        if phase in (1, 2):
+            return side * half + lax.rem(spot + off, half)
         return lax.rem(me + off, n)
 
-    def source_of(off):
+    def source_of(phase, off):
+        if phase in (1, 2):
+            return side * half + lax.rem(spot + half - off, half)
         return lax.rem(me + n - off, n)
 
     def rows(d, start):
-        return pl.ds(pl.multiple_of(lax.div(d, column_groups) * ROWS + start, ROWS), ROWS)
+        return pl.ds(pl.multiple_of(lax.div(lax.rem(d, half), column_groups) * ROWS + start, ROWS), ROWS)
 
     def columns(d, c):
         return pl.ds(pl.multiple_of(lax.rem(d, column_groups) * share[c], LANES), share[c])
@@ -70,7 +77,7 @@
         if phase == 0:
             return own[c].at[0, rows(d, 0), columns(d, c)]
         if phase == 1:
-            return stage[c].at[d]
+            return stage[c].at[lax.rem(d, half)]
         if phase == 2:
             return term[c].at[:, rows(d, base[c]), columns(d, c)]
         return sums[c].at[d]
@@ -81,59 +88,61 @@
         if phase == 1:
             return tile[c].at[:, rows(d, base[c]), columns(d, c)]
         if phase == 2:
-            return recv[c].at[d]
-        return out[c].at[0, rows(d, 0), columns(d, c)]
-
-    def each_peer(body):
+            return recv[c].at[lax.rem(d, half)]
+        return home[c].at[lax.div(d, half), rows(d, 0), columns(d, c)]
+
+    def each_peer(phase, body):
         def step(off, carry):
             body(off)
             return carry
 
-        lax.fori_loop(1, n, step, 0)
+        lax.fori_loop(1, half if phase in (1, 2) else n, step, 0)
 
     def send(phase, c):
-        each_peer(
-            lambda off: remote(
-                source(phase, c, peer_of(off)), target(phase, c, me), phase, c, off, peer_of(off)
-            ).start()
-        )
+        def step(off):
+            peer = peer_of(phase, off)
+            remote(source(phase, c, peer), target(phase, c, me), phase, c, off, peer).start()
+
+        each_peer(phase, step)
         pltpu.make_async_copy(source(phase, c, me), target(phase, c, me), own_sem.at[phase, c]).start()
 
     def arrive(phase, c):
         pltpu.make_async_copy(source(phase, c, me), target(phase, c, me), own_sem.at[phase, c]).wait()
-        each_peer(
-            lambda off: remote(
-                source(phase, c, me), target(phase, c, source_of(off)), phase, c, off, peer_of(off)
-            ).wait_recv()
-        )
+
+        def step(off):
+            landed = target(phase, c, source_of(phase, off))
+            remote(source(phase, c, me), landed, phase, c, off, peer_of(phase, off)).wait_recv()
+
+        each_peer(phase, step)
 
     def drain(phase, c):
-        each_peer(
-            lambda off: remote(
-                source(phase, c, peer_of(off)), target(phase, c, me), phase, c, off, peer_of(off)
-            ).wait_send()
-        )
+        def step(off):
+            peer = peer_of(phase, off)
+            remote(source(phase, c, peer), target(phase, c, me), phase, c, off, peer).wait_send()
+
+        each_peer(phase, step)
 
     def id_copy(off, slot):
         return pltpu.make_async_remote_copy(
             src_ref=ids_ref, dst_ref=ids_v.at[slot],
             send_sem=id_send.at[off], recv_sem=id_recv.at[off],
-            device_id=(group, peer_of(off)), device_id_type=pl.DeviceIdType.MESH,
+            device_id=(group, peer_of(0, off)), device_id_type=pl.DeviceIdType.MESH,
         )
 
     barrier = pltpu.get_barrier_semaphore()
     each_peer(
+        0,
         lambda off: pl.semaphore_signal(
-            barrier, inc=1, device_id=(group, peer_of(off)), device_id_type=pl.DeviceIdType.MESH
-        )
+            barrier, inc=1, device_id=(group, peer_of(0, off)), device_id_type=pl.DeviceIdType.MESH
+        ),
     )
     pl.semaphore_wait(barrier, n - 1)
 
-    each_peer(lambda off: id_copy(off, me).start())
+    each_peer(0, lambda off: id_copy(off, me).start())
     for c in (QD, VD, QU, VU):
         send(0, c)
     ids_v[me] = ids_ref[...]
-    each_peer(lambda off: id_copy(off, source_of(off)).wait_recv())
+    each_peer(0, lambda off: id_copy(off, source_of(0, off)).wait_recv())
     fetch = pltpu.make_async_copy(ids_v, ids_s, id_recv.at[0])
     fetch.start()
     fetch.wait()
@@ -141,20 +150,20 @@
     def pick(c):
         def step(d, carry):
             for k in range(per_dev):
-                stage[c][d, k] = hold[c][ids_s[d, k, 0]]
-            return carry
-
-        lax.fori_loop(0, n, step, 0)
+                stage[c][d, k] = hold[c][ids_s[side * half + d, k, 0]]
+            return carry
+
+        lax.fori_loop(0, half, step, 0)
 
     for c in (QD, VD, QU, VU):
         arrive(0, c)
         pick(c)
         send(1, c)
 
-    blocks = n * per_dev
+    blocks = half * per_dev
 
     def id_of(b):
-        return ids_s[lax.div(b, per_dev), lax.rem(b, per_dev), 0]
+        return ids_s[side * half + lax.div(b, per_dev), lax.rem(b, per_dev), 0]
 
     def find_prev(b, carry):
         mine = id_of(b)
@@ -247,13 +256,24 @@
         arrive(2, c)
         reduce(c)
         send(3, c)
-    each_peer(lambda off: id_copy(off, me).wait_send())
+    each_peer(0, lambda off: id_copy(off, me).wait_send())
     for phase in range(3):
         for c in range(4):
             drain(phase, c)
     for c in (QU, VU, QD, VD):
         arrive(3, c)
         drain(3, c)
+        count, size = slabs(widths[c])
+
+        def add(i, carry):
+            cols = pl.ds(pl.multiple_of(i * size, LANES), size)
+            total = home[c][0, :, cols].astype(jnp.float32)
+            for h in range(1, n // half):
+                total += home[c][h, :, cols].astype(jnp.float32)
+            out[c][0, :, cols] = total.astype(jnp.bfloat16)
+            return carry
+
+        lax.fori_loop(0, count, add, 0)
 
 
 def per_device(
@@ -263,7 +283,8 @@
     rows, width = inputs.shape
     per_dev = rows // BLOCK
     rank = query_down.shape[1]
-    column_groups = n // (rank // ROWS)
+    half = n // 2
+    column_groups = half // (rank // ROWS)
 
     def padded(w):
         return column_groups * max(LANES, w // column_groups)
@@ -293,7 +314,7 @@
         jnp.broadcast_to(block_adapter, (per_dev, LANES)), ((0, -per_dev % 8), (0, 0))
     )
     bf, f32 = jnp.bfloat16, jnp.float32
-    blocks = n * per_dev
+    blocks = half * per_dev
     scratch = [
         pltpu.VMEM((n,) + ids.shape, jnp.int32),
         pltpu.SMEM((n,) + ids.shape, jnp.int32),
@@ -301,15 +322,16 @@
         pltpu.SMEM((n,), jnp.int32),
     ]
     scratch += [pltpu.VMEM((n, ROWS, s), bf) for s in share]
-    scratch += [pltpu.VMEM((n, per_dev, ROWS, s), bf) for s in share]
+    scratch += [pltpu.VMEM((half, per_dev, ROWS, s), bf) for s in share]
     for _ in range(2):
         scratch += [
             pltpu.VMEM((per_dev, 2 * rank, width), bf),
             pltpu.VMEM((per_dev, rank, qwidth), bf),
             pltpu.VMEM((per_dev, rank, vpad), bf),
         ]
-    scratch += [pltpu.VMEM((n, per_dev, ROWS, s), bf) for s in share]
+    scratch += [pltpu.VMEM((half, per_dev, ROWS, s), bf) for s in share]
     scratch += [pltpu.VMEM((n, ROWS, s), bf) for s in share]
+    scratch += [pltpu.VMEM((n // half, rank, w), bf) for w in widths]
     scratch += [
         pltpu.VMEM((blocks + 1, ROWS, share[QU]), f32),
         pltpu.VMEM((blocks + 1, ROWS, share[VU]), f32),
@@ -322,7 +344,7 @@
     ]
     vmem = pl.BlockSpec(memory_space=pltpu.VMEM)
     grad, qdown, vdown, qup, vup = pl.pallas_call(
-        functools.partial(kernel, n, rank, per_dev, widths),
+        functools.partial(kernel, n, half, rank, per_dev, widths),
         out_shape=(
             jax.ShapeDtypeStruct((per_dev, BLOCK, width), bf),
             jax.ShapeDtypeStruct((1, rank, width), bf),

time: 244 us -> 212 us (0.87); the launches traced: 242 us -> 212 us
  Pallas kernels: 233 us -> 204 us
    pallas_call x1, Pallas kernels: 233 us -> 204 us  [per_device(): pl.pallas_call(functools.partial(kernel, n, half, rank, per_dev, widths),...]
where the time goes in v1:
time: 212 us
  Pallas kernels  204 us (96%)
  local copies, waits for them, and re-layouts  7.8 us (4%)
    pallas_call x1, Pallas kernels, per_device(): pl.pallas_call(functools.partial(kernel, n, half, rank, per_dev, widths),...  204 us
    unnamed x7, local copies, waits for them, and re-layouts  7.07 us

profile of v1, /device:TPU:0, one launch (start us, length us, event | category | flops | bytes accessed | tf_op | source)
XLA Modules:
  0.0 212.3 jit_solution(13623282174734328735)
XLA Ops:
  0.6 0.7 pad.6
  1.3 0.1 pad.7.ids_ref
  1.4 0.0 copy-start
  1.4 0.9 copy-done
  2.3 203.8 %shard_map.119 = (bf16[2,128,4096]{2,1,0:T(8,128)(2,1)}, bf16[1,64,4096]{2,1,0:T(8,128)(2,1)S(1)}, bf16[1,64,4096]{2,1,0:T(8,128)(2,1)S(1)}, bf16[1,64,4096]{2,1,0:T(8,128)(2,1)S(1)}, bf16[1,64,1024]{2,1,0:T(8,128)(2,1)S(1)}) custom-call(s32[8,128]{1,0:T(8,128)S(1)} %pad.7.ids_ref, bf16[2,128,4096]{2,1,0:T(8,128)(2,1)} %bitcast.6, ...), custom_call_target="tpu_custom_call" | custom-call | tf_op jit(solution)/shard_map/pallas_call | solution.py:346
  206.1 3.1 %copy.18 = bf16[256,4096]{1,0:T(8,128)(2,1)} copy(bf16[256,4096]{1,0:T(8,128)(2,1)} %bitcast.5) | data formatting | bytes 4194304
  209.2 0.8 copy.19
  210.0 0.8 copy.20
  210.8 0.8 copy.21
  211.6 0.7 copy.22
Async XLA Ops:
  1.4 0.9 copy-start

commit v2 on v1

--- a/solution.py
+++ b/solution.py
@@ -139,8 +139,8 @@
     pl.semaphore_wait(barrier, n - 1)
 
     each_peer(0, lambda off: id_copy(off, me).start())
-    for c in (QD, VD, QU, VU):
-        send(0, c)
+    send(0, QD)
+    send(0, VD)
     ids_v[me] = ids_ref[...]
     each_peer(0, lambda off: id_copy(off, source_of(0, off)).wait_recv())
     fetch = pltpu.make_async_copy(ids_v, ids_s, id_recv.at[0])
@@ -159,6 +159,8 @@
         arrive(0, c)
         pick(c)
         send(1, c)
+        if c + 2 <= VU:
+            send(0, c + 2)
 
     blocks = half * per_dev
 
@@ -198,7 +200,7 @@
             0, count, step, jnp.zeros((tile_ref.shape[1], BLOCK), jnp.float32)
         )
 
-    def expand(left, token_ref, k, target_ref, scale):
+    def expand(left, token_ref, k, target_ref, scale, start=0):
         count, size = slabs(token_ref.shape[2])
 
         def step(i, carry):
@@ -206,7 +208,7 @@
             value = dot(left, token_ref[k, :, cols], ((1,), (0,)))
             if scale is not None:
                 value = scale * value
-            target_ref[k, :, cols] = value.astype(jnp.bfloat16)
+            target_ref[k, pl.ds(start, left.shape[0]), cols] = value.astype(jnp.bfloat16)
             return carry
 
         lax.fori_loop(0, count, step, 0)
@@ -219,15 +221,6 @@
         expand(low[rank:], vc_ref, k, term_vu, adapter_scale)
     send(2, QU)
     send(2, VU)
-    arrive(1, QU)
-    arrive(1, VU)
-    for k in range(per_dev):
-        back_s[k, :rank] = adapter_scale * contract(tile_qu, k, qc_ref)
-        back_s[k, rank:] = adapter_scale * contract(tile_vu, k, vc_ref)
-        expand(back_s[k].astype(jnp.bfloat16), x_ref, k, term_d, None)
-    send(2, QD)
-    send(2, VD)
-
     def reduce(c):
         s = chains[c]
         s[0] = jnp.zeros(s.shape[1:], jnp.float32)
@@ -245,17 +238,28 @@
 
         lax.fori_loop(0, n, close, 0)
 
-    for c in (QU, VU):
+    def backward(c, up, cot_ref):
+        arrive(1, up)
+        for k in range(per_dev):
+            back = adapter_scale * contract(tile[up], k, cot_ref)
+            back_s[k, pl.ds(base[c], rank)] = back
+            expand(back.astype(jnp.bfloat16), x_ref, k, term_d, None, base[c])
+        send(2, c)
+
+    def total(c):
         arrive(2, c)
         reduce(c)
         send(3, c)
+
+    backward(QD, QU, qc_ref)
+    total(QU)
+    backward(VD, VU, vc_ref)
+    total(VU)
+    total(QD)
     for k in range(per_dev):
         back = back_s[k].T.astype(jnp.bfloat16)
         expand(back, tile_d, k, grad_ref, None)
-    for c in (QD, VD):
-        arrive(2, c)
-        reduce(c)
-        send(3, c)
+    total(VD)
     each_peer(0, lambda off: id_copy(off, me).wait_send())
     for phase in range(3):
         for c in range(4):

time: 212 us -> 215 us (1.014)
  no operation moved by 1% of the time
where the time goes in v2:
time: 215 us; the launch traced here: 214 us
  Pallas kernels  205 us (95%)
  local copies, waits for them, and re-layouts  7.8 us (4%)
    pallas_call x1, Pallas kernels, per_device(): pl.pallas_call(functools.partial(kernel, n, half, rank, per_dev, widths),...  205 us
    unnamed x7, local copies, waits for them, and re-layouts  7.07 us

profile of v2, /device:TPU:0, one launch (start us, length us, event | category | flops | bytes accessed | tf_op | source)
XLA Modules:
  0.0 213.7 jit_solution(10295381759351838230)
XLA Ops:
  0.6 0.7 pad.6
  1.3 0.1 pad.7.ids_ref
  1.4 0.0 copy-start
  1.4 0.9 copy-done
  2.3 205.3 %shard_map.119 = (bf16[2,128,4096]{2,1,0:T(8,128)(2,1)}, bf16[1,64,4096]{2,1,0:T(8,128)(2,1)S(1)}, bf16[1,64,4096]{2,1,0:T(8,128)(2,1)S(1)}, bf16[1,64,4096]{2,1,0:T(8,128)(2,1)S(1)}, bf16[1,64,1024]{2,1,0:T(8,128)(2,1)S(1)}) custom-call(s32[8,128]{1,0:T(8,128)S(1)} %pad.7.ids_ref, bf16[2,128,4096]{2,1,0:T(8,128)(2,1)} %bitcast.6, ...), custom_call_target="tpu_custom_call" | custom-call | tf_op jit(solution)/shard_map/pallas_call | solution.py:350
  207.6 3.1 %copy.18 = bf16[256,4096]{1,0:T(8,128)(2,1)} copy(bf16[256,4096]{1,0:T(8,128)(2,1)} %bitcast.5) | data formatting | bytes 4194304
  210.7 0.8 copy.19
  211.5 0.8 copy.20
  212.3 0.8 copy.21
  213.1 0.7 copy.22
Async XLA Ops:
  1.4 0.9 copy-start

commit v3 on v1

--- a/solution.py
+++ b/solution.py
@@ -1,4 +1,5 @@
 import functools
+import math
 
 import jax
 import jax.numpy as jnp
@@ -50,15 +51,18 @@
     chains = (chain, chain, chain, chain_v)
     base = (0, rank, 0, 0)
 
+    stride = next(s for s in range(n // 3, 0, -1) if math.gcd(s, n) == 1)
+    near_stride = next(s for s in range(half // 2, 0, -1) if math.gcd(s, half) == 1)
+
     def peer_of(phase, off):
         if phase in (1, 2):
-            return side * half + lax.rem(spot + off, half)
-        return lax.rem(me + off, n)
+            return side * half + lax.rem(spot + off * near_stride, half)
+        return lax.rem(me + off * stride, n)
 
     def source_of(phase, off):
         if phase in (1, 2):
-            return side * half + lax.rem(spot + half - off, half)
-        return lax.rem(me + n - off, n)
+            return side * half + lax.rem(spot + half * near_stride - off * near_stride, half)
+        return lax.rem(me + n * stride - off * stride, n)
 
     def rows(d, start):
         return pl.ds(pl.multiple_of(lax.div(lax.rem(d, half), column_groups) * ROWS + start, ROWS), ROWS)

time: 212 us -> 213 us (level)
  no operation moved by 1% of the time
where the time goes in v3:
time: 213 us; the launch traced here: 212 us
  Pallas kernels  203 us (95%)
  local copies, waits for them, and re-layouts  7.8 us (4%)
    pallas_call x1, Pallas kernels, per_device(): pl.pallas_call(functools.partial(kernel, n, half, rank, per_dev, widths),...  203 us
    unnamed x7, local copies, waits for them, and re-layouts  7.07 us

profile of v3, /device:TPU:0, one launch (start us, length us, event | category | flops | bytes accessed | tf_op | source)
XLA Modules:
  0.0 211.8 jit_solution(15037268885848980649)
XLA Ops:
  0.6 0.7 pad.6
  1.3 0.1 pad.7.ids_ref
  1.4 0.0 copy-start
  1.4 0.9 copy-done
  2.3 203.3 %shard_map.119 = (bf16[2,128,4096]{2,1,0:T(8,128)(2,1)}, bf16[1,64,4096]{2,1,0:T(8,128)(2,1)S(1)}, bf16[1,64,4096]{2,1,0:T(8,128)(2,1)S(1)}, bf16[1,64,4096]{2,1,0:T(8,128)(2,1)S(1)}, bf16[1,64,1024]{2,1,0:T(8,128)(2,1)S(1)}) custom-call(s32[8,128]{1,0:T(8,128)S(1)} %pad.7.ids_ref, bf16[2,128,4096]{2,1,0:T(8,128)(2,1)} %bitcast.6, ...), custom_call_target="tpu_custom_call" | custom-call | tf_op jit(solution)/shard_map/pallas_call | solution.py:350
  205.6 3.1 %copy.18 = bf16[256,4096]{1,0:T(8,128)(2,1)} copy(bf16[256,4096]{1,0:T(8,128)(2,1)} %bitcast.5) | data formatting | bytes 4194304
  208.7 0.8 copy.19
  209.5 0.8 copy.20
  210.3 0.8 copy.21
  211.1 0.7 copy.22
Async XLA Ops:
  1.4 0.9 copy-start

commit v4 on v1

--- a/solution.py
+++ b/solution.py
@@ -21,8 +21,8 @@
 
 def kernel(
     n, half, rank, per_dev, widths,
-    ids_ref, x_ref, qc_ref, vc_ref, qd_ref, vd_ref, qu_ref, vu_ref,
-    grad_ref, oqd_ref, ovd_ref, oqu_ref, ovu_ref,
+    ids_ref, x_hbm, qc_hbm, vc_hbm, qd_ref, vd_ref, qu_ref, vu_ref,
+    grad_hbm, oqd_ref, ovd_ref, oqu_ref, ovu_ref,
     ids_v, ids_s, prev_s, last_s,
     hold_qd, hold_vd, hold_qu, hold_vu,
     stage_qd, stage_vd, stage_qu, stage_vu,
@@ -32,6 +32,7 @@
     home_qd, home_vd, home_qu, home_vu,
     chain, chain_v, back_s,
     send_sem, recv_sem, id_send, id_recv, own_sem,
+    x_ref, qc_ref, vc_ref, grad_ref, local_sem,
 ):
     group, me = lax.axis_index("groups"), lax.axis_index("dev")
     row_groups = rank // ROWS
@@ -129,6 +130,12 @@
             device_id=(group, peer_of(0, off)), device_id_type=pl.DeviceIdType.MESH,
         )
 
+    loads = [
+        pltpu.make_async_copy(src, dst, local_sem.at[i])
+        for i, (src, dst) in enumerate(((x_hbm, x_ref), (qc_hbm, qc_ref), (vc_hbm, vc_ref)))
+    ]
+    store = pltpu.make_async_copy(grad_ref, grad_hbm, local_sem.at[3])
+
     barrier = pltpu.get_barrier_semaphore()
     each_peer(
         0,
@@ -141,6 +148,8 @@
     each_peer(0, lambda off: id_copy(off, me).start())
     for c in (QD, VD, QU, VU):
         send(0, c)
+    for load in loads:
+        load.start()
     ids_v[me] = ids_ref[...]
     each_peer(0, lambda off: id_copy(off, source_of(0, off)).wait_recv())
     fetch = pltpu.make_async_copy(ids_v, ids_s, id_recv.at[0])
@@ -211,6 +220,8 @@
 
         lax.fori_loop(0, count, step, 0)
 
+    for load in loads:
+        load.wait()
     arrive(1, QD)
     arrive(1, VD)
     for k in range(per_dev):
@@ -252,6 +263,7 @@
     for k in range(per_dev):
         back = back_s[k].T.astype(jnp.bfloat16)
         expand(back, tile_d, k, grad_ref, None)
+    store.start()
     for c in (QD, VD):
         arrive(2, c)
         reduce(c)
@@ -260,6 +272,7 @@
     for phase in range(3):
         for c in range(4):
             drain(phase, c)
+    store.wait()
     for c in (QU, VU, QD, VD):
         arrive(3, c)
         drain(3, c)
@@ -341,8 +354,14 @@
         pltpu.SemaphoreType.DMA((n,)),
         pltpu.SemaphoreType.DMA((n,)),
         pltpu.SemaphoreType.DMA((4, 4)),
+        pltpu.VMEM((per_dev, BLOCK, width), bf),
+        pltpu.VMEM((per_dev, BLOCK, qwidth), bf),
+        pltpu.VMEM((per_dev, BLOCK, vpad), bf),
+        pltpu.VMEM((per_dev, BLOCK, width), bf),
+        pltpu.SemaphoreType.DMA((4,)),
     ]
     vmem = pl.BlockSpec(memory_space=pltpu.VMEM)
+    hbm = pl.BlockSpec(memory_space=pl.ANY)
     grad, qdown, vdown, qup, vup = pl.pallas_call(
         functools.partial(kernel, n, half, rank, per_dev, widths),
         out_shape=(
@@ -352,8 +371,8 @@
             jax.ShapeDtypeStruct((1, rank, qwidth), bf),
             jax.ShapeDtypeStruct((1, rank, vpad), bf),
         ),
-        in_specs=[vmem] * 8,
-        out_specs=[vmem] * 5,
+        in_specs=[vmem] + [hbm] * 3 + [vmem] * 4,
+        out_specs=[hbm] + [vmem] * 4,
         scratch_shapes=scratch,
         compiler_params=pltpu.CompilerParams(
             collective_id=0, has_side_effects=True, vmem_limit_bytes=52 * 1024 * 1024

time: 212 us -> 210 us (level)
  Pallas kernels: 204 us -> 201 us
    pallas_call x1, Pallas kernels: 204 us -> 201 us  [per_device(): pl.pallas_call(functools.partial(kernel, n, half, rank, per_dev, widths),...]
where the time goes in v4:
time: 210 us
  Pallas kernels  201 us (96%)
  local copies, waits for them, and re-layouts  7.8 us (4%)
    pallas_call x1, Pallas kernels, per_device(): pl.pallas_call(functools.partial(kernel, n, half, rank, per_dev, widths),...  201 us
    unnamed x7, local copies, waits for them, and re-layouts  7.07 us

profile of v4, /device:TPU:0, one launch (start us, length us, event | category | flops | bytes accessed | tf_op | source)
XLA Modules:
  0.0 209.6 jit_solution(795911373119968848)
XLA Ops:
  0.6 0.7 pad.6
  1.3 0.1 pad.7.ids_ref
  1.4 0.0 copy-start
  1.4 0.9 copy-done
  2.3 201.1 %shard_map.119 = (bf16[2,128,4096]{2,1,0:T(8,128)(2,1)}, bf16[1,64,4096]{2,1,0:T(8,128)(2,1)S(1)}, bf16[1,64,4096]{2,1,0:T(8,128)(2,1)S(1)}, bf16[1,64,4096]{2,1,0:T(8,128)(2,1)S(1)}, bf16[1,64,1024]{2,1,0:T(8,128)(2,1)S(1)}) custom-call(s32[8,128]{1,0:T(8,128)S(1)} %pad.7.ids_ref, bf16[2,128,4096]{2,1,0:T(8,128)(2,1)} %bitcast.6, ...), custom_call_target="tpu_custom_call" | custom-call | tf_op jit(solution)/shard_map/pallas_call | solution.py:365
  203.4 3.1 %copy.18 = bf16[256,4096]{1,0:T(8,128)(2,1)} copy(bf16[256,4096]{1,0:T(8,128)(2,1)} %bitcast.5) | data formatting | bytes 4194304
  206.5 0.8 copy.19
  207.3 0.8 copy.20
  208.1 0.8 copy.21
  208.9 0.7 copy.22
Async XLA Ops:
  1.4 0.9 copy-start

commit v5 on v4

--- a/solution.py
+++ b/solution.py
@@ -195,16 +195,16 @@
         size = 512 if width % 512 == 0 else LANES
         return width // size, size
 
-    def contract(tile_ref, k, token_ref):
+    def contract(tile_ref, k, token_ref, start=0):
         width = token_ref.shape[2]
         count, size = slabs(width)
 
         def step(i, total):
             cols = pl.ds(pl.multiple_of(i * size, LANES), size)
-            return total + dot(tile_ref[k, :, cols], token_ref[k, :, cols], ((1,), (1,)))
+            return total + dot(tile_ref[k, pl.ds(start, rank), cols], token_ref[k, :, cols], ((1,), (1,)))
 
         return lax.fori_loop(
-            0, count, step, jnp.zeros((tile_ref.shape[1], BLOCK), jnp.float32)
+            0, count, step, jnp.zeros((rank, BLOCK), jnp.float32)
         )
 
     def expand(left, token_ref, k, target_ref, scale):
@@ -222,14 +222,12 @@
 
     for load in loads:
         load.wait()
-    arrive(1, QD)
-    arrive(1, VD)
-    for k in range(per_dev):
-        low = contract(tile_d, k, x_ref).astype(jnp.bfloat16)
-        expand(low[:rank], qc_ref, k, term_qu, adapter_scale)
-        expand(low[rank:], vc_ref, k, term_vu, adapter_scale)
-    send(2, QU)
-    send(2, VU)
+    for c, up, cot_ref in ((QD, QU, qc_ref), (VD, VU, vc_ref)):
+        arrive(1, c)
+        for k in range(per_dev):
+            low = contract(tile_d, k, x_ref, base[c]).astype(jnp.bfloat16)
+            expand(low, cot_ref, k, term[up], adapter_scale)
+        send(2, up)
     arrive(1, QU)
     arrive(1, VU)
     for k in range(per_dev):

time: 210 us -> 210 us (level)
  no operation moved by 1% of the time
where the time goes in v5:
time: 210 us; the launch traced here: 209 us
  Pallas kernels  201 us (96%)
  local copies, waits for them, and re-layouts  7.8 us (4%)
    pallas_call x1, Pallas kernels, per_device(): pl.pallas_call(functools.partial(kernel, n, half, rank, per_dev, widths),...  201 us
    unnamed x7, local copies, waits for them, and re-layouts  7.07 us

profile of v5, /device:TPU:0, one launch (start us, length us, event | category | flops | bytes accessed | tf_op | source)
XLA Modules:
  0.0 209.3 jit_solution(11474179081392574371)
XLA Ops:
  0.6 0.7 pad.6
  1.3 0.1 pad.7.ids_ref
  1.4 0.0 copy-start
  1.4 0.9 copy-done
  2.3 200.9 %shard_map.119 = (bf16[2,128,4096]{2,1,0:T(8,128)(2,1)}, bf16[1,64,4096]{2,1,0:T(8,128)(2,1)S(1)}, bf16[1,64,4096]{2,1,0:T(8,128)(2,1)S(1)}, bf16[1,64,4096]{2,1,0:T(8,128)(2,1)S(1)}, bf16[1,64,1024]{2,1,0:T(8,128)(2,1)S(1)}) custom-call(s32[8,128]{1,0:T(8,128)S(1)} %pad.7.ids_ref, bf16[2,128,4096]{2,1,0:T(8,128)(2,1)} %bitcast.6, ...), custom_call_target="tpu_custom_call" | custom-call | tf_op jit(solution)/shard_map/pallas_call | solution.py:363
  203.2 3.1 %copy.18 = bf16[256,4096]{1,0:T(8,128)(2,1)} copy(bf16[256,4096]{1,0:T(8,128)(2,1)} %bitcast.5) | data formatting | bytes 4194304
  206.3 0.8 copy.19
  207.1 0.8 copy.20
  207.9 0.8 copy.21
  208.7 0.7 copy.22
Async XLA Ops:
  1.4 0.9 copy-start
